TPU v7x, 32 devices: a whole 2x2x4 slice. The times are simulated.
32 devices in a mesh: prow: 8 (over z, x), pcol: 4 (over y, core).
Axes of the slice: x: 2, y: 2, z: 4, core: 2. Of those that a mesh axis runs over, the one named last changes fastest.
Arguments:
- slab: float32 [4096, 2048], P('prow', 'pcol'), may hold values from -6 to 6
- panel: float32 [4096, 512], P('prow', 'pcol'), may hold values from -0.25 to 0.25
- tri_inverse: float32 [512, 512], replicated, as said below
- pivots: int32 [512], replicated, may hold values from 512 to 4095, as said below
Outputs:
- updated: float32 [4096, 2048], P('prow', 'pcol')
Inputs may be any that keep to these rules, and one draw needn't show every extreme that they name: The pivots are distinct row numbers of the rows below the first 512. At most 75 of them fall among the 512 rows of one device, and some device holds exactly 75. `tri_inverse`: lower triangular with zeros above the diagonal; the diagonal lies between 0.8 and 1.2.
All inputs are finite; a program needn't handle non-finite values.
Results may differ from a plain program's by a relative error of at most 0.000053.
Values sent between devices are 32-bit elements; how exact they have to be, the bound alone decides.
No kernel may reach another device: no remote copies, remote signals or barrier semaphores. Data moves between devices by JAX's collectives and lax.ppermute only.
A program may use at most 64 MiB of HBM per device.

v0:
```python
import jax
import jax.numpy as jnp
from jax import lax
from jax.sharding import PartitionSpec as P


def per_device(slab, panel, tri_inverse, pivots):
    rows_dev = slab.shape[0]
    cols_dev = slab.shape[1]
    count_rows = lax.axis_size("prow")
    my_row = lax.axis_index("prow")
    owner_row = pivots // rows_dev
    local_row = pivots - owner_row * rows_dev
    is_owned = owner_row == my_row
    picked = jnp.where(is_owned[:, None], slab[local_row], 0.0)
    target = jnp.where(is_owned, local_row, rows_dev)
    capacity = rows_dev // (count_rows - 1) + 2
    count_piv = pivots.shape[0]
    same_owner = owner_row[:, None] == owner_row[None, :]
    earlier = jnp.arange(count_piv)[None, :] < jnp.arange(count_piv)[:, None]
    position = jnp.sum(same_owner & earlier, axis=1)
    slot_index = owner_row * capacity + position
    buffer = jnp.zeros((count_rows * capacity, cols_dev), jnp.float32).at[slot_index].set(slab)
    outgoing = jnp.where(my_row == 0, buffer, 0.0)
    received = lax.all_to_all(outgoing, "prow", split_axis=0, concat_axis=0, tiled=True)
    placed = received[position]
    swapped = slab.at[target].set(placed, mode="drop")
    rows_u = lax.psum(picked, "prow")
    u_block = jnp.dot(
        tri_inverse, rows_u, precision=lax.Precision.HIGHEST, preferred_element_type=jnp.float32
    )
    product = jnp.dot(
        lax.all_gather(panel, "pcol", axis=1, tiled=True),
        u_block,
        precision=lax.Precision.HIGHEST,
        preferred_element_type=jnp.float32,
    )
    updated = swapped - product
    return jnp.where(my_row == 0, u_block, updated)


def solution(mesh):
    return jax.shard_map(
        per_device,
        mesh=mesh,
        in_specs=(P("prow", "pcol"), P("prow", "pcol"), P(), P()),
        out_specs=P("prow", "pcol"),
        check_vma=False,
    )
```

profile of v0, /device:TPU:0, one launch (start us, length us, event | category | flops | bytes accessed | tf_op | source)
XLA Modules:
  0.0 135.4 jit_solution(12268747893432640873)
XLA Ops:
  7.4 0.0 copy-start
  7.4 0.0 copy-start.2
  7.4 0.0 all-reduce.2.cloned.1.call-start
  7.4 1.3 copy.14
  8.7 0.0 copy-done.2
  8.7 0.2 convert_reduce_fusion
  9.0 1.6 %gather_fusion = f32[512,512]{1,0:T(8,128)S(1)} fusion(f32[512,512]{1,0:T(8,128)S(1)} %copy.14, s32[1024]{0:T(1024)S(1)} %pad_clamp_fusion.1), kind=kCustom, calls=%fused_computation | custom fusion | bytes 2099200 | tf_op jit(solution)/shard_map/gather | solution.py:15
  10.6 1.1 broadcast_select_fusion.1
  11.7 0.0 all-reduce.2.cloned.1.call-update
  11.8 2.5 %scatter_custom_fusion = f32[600,512]{1,0:T(8,128)S(1)} fusion(s32[512]{0:T(512)S(1)} %get-tuple-element.9, f32[512,512]{1,0:T(8,128)S(1)} %copy.14, f32[]{:T(128)} %constant.30.clone.1), kind=kCustom, calls=%fused_computation.13 | custom fusion | bytes 1228804 | tf_op jit(solution)/shard_map/scatter | solution.py:23
  14.3 1.2 broadcast_select_fusion
  15.5 2.5 %all_to_all.8 = f32[8,75,512]{2,1,0:T(8,128)} reshape(f32[600,512]{1,0:T(8,128)} %broadcast_select_fusion) | data formatting | bytes 2457600 | tf_op jit(solution)/shard_map/all_to_all | solution.py:25
  18.0 7.3 %all-to-all-start = ((f32[8,75,512]{2,1,0:T(8,128)}), f32[8,75,512]{2,1,0:T(8,128)S(1)}, u32[]{:S(2)}, u32[]{:S(2)}) async-start(f32[8,75,512]{2,1,0:T(8,128)} %all_to_all.8), calls=%async_computation | async-start | bytes 2621440 | tf_op jit(solution)/shard_map/all_to_all | solution.py:25
  25.2 0.0 all-gather.2.cloned.1.call-start
  25.3 0.5 all-gather.2.cloned.1.call-update
  25.8 82.8 %all-reduce.2.cloned.1.call-done = f32[512,512]{1,0:T(8,128)} async-done(((f32[512,512]{1,0:T(8,128)}), f32[512,512]{1,0:T(8,128)}) %all-reduce.2.cloned.1.call-update) | async-done | bytes 1048592 | tf_op jit(solution)/shard_map/psum | solution.py:28
  108.7 0.0 copy-done
  108.7 5.7 %fusion.9 = f32[512,512]{1,0:T(8,128)} fusion(f32[512,512]{1,0:T(8,128)} %all-reduce.2.cloned.1.call-done, f32[512,512]{1,0:T(8,128)S(1)} %copy-done), kind=kOutput, calls=%fused_computation.31 | convolution fusion | flops 1610612736 | bytes 3145728 | tf_op jit(solution)/shard_map/dot_general | solution.py:29
  114.3 0.0 all-to-all-done
  114.3 1.2 all_to_all.10
  115.5 6.3 %scatter_custom_fusion.1 = f32[512,512]{1,0:T(8,128)S(1)} fusion(f32[512,512]{1,0:T(8,128)S(1)} %copy.14, s32[512]{0:T(512)S(1)} %get-tuple-element.7, f32[600,512]{1,0:T(8,128)} %all_to_all.10, s32[1024]{0:T(1024)S(1)} %pad_clamp_fusion), kind=kCustom, calls=%fused_computation.7 | custom fusion | bytes 1048576 | tf_op jit(solution)/shard_map/scatter | solution.py:27
  121.9 0.0 copy-start.1
  121.9 1.3 copy.9
  123.2 0.0 all-gather.2.cloned.1.call-done
  123.2 0.0 copy-done.1
  123.2 3.4 %fusion.1 = f32[512,512]{0,1:T(8,128)S(1)} fusion(f32[512,512]{0,1:T(8,128)} %copy.9, f32[512,512]{1,0:T(8,128)S(1)} %copy-done.1, f32[512,512]{1,0:T(8,128)} %all-gather.2.cloned.1.call-done, pred[]{:T(512)S(6)} %eq.23), kind=kOutput, calls=%fused_computation.6 | convolution fusion | flops 1611137024 | bytes 4194305 | tf_op jit(solution)/shard_map/dot_general | solution.py:32
  126.6 1.3 copy.10
  (5 shorter events, 0.0 us)
Async XLA Ops:
  7.4 101.3 %copy-start = (f32[512,512]{1,0:T(8,128)S(1)}, f32[512,512]{1,0:T(8,128)}, u32[]{:S(2)}) copy-start(f32[512,512]{1,0:T(8,128)} %param.6) | copy-start | bytes 3145732
  7.4 1.3 copy-start.2
  7.4 101.3 %all-reduce.2.cloned.1.call-start = ((), (), s32[]{:S(2)}) async-start(), calls=%async_computation.1 | async-start | bytes 2097152 | tf_op jit(solution)/shard_map/psum | solution.py:28
  18.0 96.4 %all-to-all-start = ((f32[8,75,512]{2,1,0:T(8,128)}), f32[8,75,512]{2,1,0:T(8,128)S(1)}, u32[]{:S(2)}, u32[]{:S(2)}) async-start(f32[8,75,512]{2,1,0:T(8,128)} %all_to_all.8), calls=%async_computation | async-start | bytes 2621440 | tf_op jit(solution)/shard_map/all_to_all | solution.py:25
  25.2 98.0 %all-gather.2.cloned.1.call-start = ((), (), s32[]{:S(2)}) async-start(), calls=%async_computation.2 | async-start | bytes 1310720 | tf_op jit(solution)/shard_map/all_gather | solution.py:33
  121.9 1.3 copy-start.1
Sparse Core Ops, SparseCore 0:
  11.9 96.7 all-reduce.1
Sparse Core Ops, SparseCore 1:
  27.3 18.1 all-gather.1
where the time goes:
time: 136 us; the launch traced here: 135 us
  waiting for transfers between devices  83.4 us (61%)
  local copies, waits for them, and re-layouts  18.1 us (13%)
  between operations  14.9 us (11%)
  matrix products  9.06 us (7%)
  starting transfers between devices  7.29 us (5%)
  other arithmetic  2.57 us (2%)
    psum x1, waiting for transfers between devices, per_device(): rows_u = lax.psum(picked, 'prow')  82.8 us
    scatter x2, local copies, waits for them, and re-layouts, per_device(): swapped = slab.at[target].set(placed, mode='drop')  7.65 us
    all_to_all x1, starting transfers between devices, per_device(): lax.all_to_all(outgoing, 'prow', split_axis=0, concat_axis=0, tiled=True)  7.25 us
    dot_general x1, matrix products, per_device(): jnp.dot(tri_inverse, rows_u, precision=lax.Precision.HIGHEST, preferred_e...  5.66 us
    all_to_all x2, local copies, waits for them, and re-layouts, per_device(): lax.all_to_all(outgoing, 'prow', split_axis=0, concat_axis=0, tiled=True)  3.69 us
    dot_general x1, matrix products, per_device(): jnp.dot(lax.all_gather(panel, 'pcol', axis=1, tiled=True), u_block, preci...  3.4 us
  transfers between devices with their start and end apart: 3, of which 1 were waited for; matrix products, arithmetic and copies ran while one was open for 13% of the time, Pallas kernels for 0%

commit v1 on v0

v1 whole, which is shorter than its diff:
```python
import functools

import jax
import jax.numpy as jnp
from jax import lax
from jax.experimental import pallas as pl
from jax.experimental.pallas import tpu as pltpu
from jax.sharding import PartitionSpec as P

F32 = jnp.float32
BF16 = jnp.bfloat16
VMEM_BYTES = 48 * 1024 * 1024


def _two_parts(x):
    high = x.astype(BF16)
    low = (x - high.astype(F32)).astype(BF16)
    return high, low


def _three_parts(x):
    high = x.astype(BF16)
    rest = x - high.astype(F32)
    mid = rest.astype(BF16)
    low = (rest - mid.astype(F32)).astype(BF16)
    return high, mid, low


def _dot(a, b):
    return jnp.dot(a, b, preferred_element_type=F32)


def _dot_nt(a, b):
    return lax.dot_general(a, b, (((1,), (1,)), ((), ())), preferred_element_type=F32)


def _iota(shape, dim):
    return lax.broadcasted_iota(jnp.int32, shape, dim)


def _owners_and_ranks(piv, rows_dev, devices):
    count = piv.shape[1]
    owner = piv // rows_dev
    local = piv - owner * rows_dev
    is_owner = _iota((devices, count), 0) == owner
    earlier = (_iota((count, count), 0) < _iota((count, count), 1)).astype(BF16)
    ranks = _dot(is_owner.astype(BF16), earlier)
    rank = jnp.sum(jnp.where(is_owner, ranks, 0.0), axis=0, keepdims=True)
    return owner, local, rank.astype(jnp.int32)


def _select_rows(one_hot, parts):
    high, mid, low = parts
    return (_dot(one_hot, high) + _dot(one_hot, mid)) + _dot(one_hot, low)


def _outgoing_kernel(devices, block, me_ref, piv_ref, slab_ref, *out_refs):
    me = me_ref[0]
    rows_dev = slab_ref.shape[0]
    piv = piv_ref[...]
    count = piv.shape[1]
    owner, local, rank = _owners_and_ranks(piv, rows_dev, devices)
    parts = _three_parts(slab_ref[...])

    @pl.when(me == 0)
    def _():
        for step in range(1, devices):
            slot = jnp.where(owner == step, rank, -1)
            pick = (_iota((block, count), 0) == slot).astype(BF16)
            if count < rows_dev:
                pick = jnp.pad(pick, ((0, 0), (0, rows_dev - count)))
            out_refs[step][...] = _select_rows(pick, parts)
        out_refs[0][...] = jnp.zeros_like(out_refs[0])

    @pl.when(me != 0)
    def _():
        slot = jnp.where(owner == me, rank, -1)
        pick = (_iota((block, count), 0) == slot).astype(BF16)
        at_row = (_iota((rows_dev, count), 0) == local).astype(BF16)
        mine = _select_rows(_dot_nt(pick, at_row).astype(BF16), parts)
        for step in range(devices):
            out_refs[step][...] = mine


def _factor_kernel(devices, block, pieces, me_ref, col_ref, piv_ref, slab_ref, tri_ref, *refs):
    panel_refs = refs[:pieces]
    high_ref, low_ref, kept_ref, w_ref = refs[pieces:]
    me = me_ref[0]
    rows_dev = slab_ref.shape[0]
    depth = panel_refs[0].shape[1]
    piv = piv_ref[...]
    count = piv.shape[1]
    owner, local, rank = _owners_and_ranks(piv, rows_dev, devices)

    @pl.when(me == 0)
    def _():
        w_ref[...] = tri_ref[...]

    @pl.when(me != 0)
    def _():
        for step in range(pieces):
            first = pl.multiple_of((col_ref[0] ^ step) * depth, depth)
            tri_high, tri_low = _two_parts(tri_ref[pl.ds(first, depth), :])
            high, low = _two_parts(panel_refs[step][...])
            term = (_dot(high, tri_low) + _dot(low, tri_high)) + _dot(high, tri_high)
            if step == 0:
                w_ref[...] = -term
            else:
                w_ref[...] -= term

    total = devices * block
    slot = (owner ^ me) * block + rank
    place = (_iota((total, count), 0) == slot).astype(BF16)
    is_mine = owner == me
    lead_slot = jnp.where(is_mine, me * block + rank, -1)
    lead = (_iota((total, count), 0) == lead_slot).astype(BF16)
    at_row = ((_iota((rows_dev, count), 0) == local) & is_mine).astype(F32)
    high, low = _two_parts(w_ref[...])
    high_ref[...] = (_dot_nt(high, place) + _dot_nt(at_row.astype(BF16), lead)).astype(BF16)
    low_ref[...] = _dot_nt(low, place).astype(BF16)
    taken = jnp.sum(at_row, axis=1, keepdims=True)
    stays = (taken < 0.5) & (me != 0)
    kept_ref[...] = jnp.where(stays, slab_ref[...], 0.0)


def _update_kernel(devices, block, high_ref, low_ref, kept_ref, *refs):
    block_refs = refs[:devices]
    out_ref, high_rows, low_rows = refs[devices:]
    for step in range(devices):
        high, low = _two_parts(block_refs[step][...])
        high_rows[pl.ds(step * block, block), :] = high
        low_rows[pl.ds(step * block, block), :] = low
    small = _dot(high_ref[...], low_rows[...]) + _dot(low_ref[...], high_rows[...])
    out_ref[...] = kept_ref[...] + (small + _dot(high_ref[...], high_rows[...]))


def _whole(memory=pltpu.VMEM):
    return pl.BlockSpec(memory_space=memory)


def per_device(slab, panel, tri_inverse, pivots):
    rows_dev, cols_dev = slab.shape
    depth = panel.shape[1]
    count = pivots.shape[0]
    devices = lax.axis_size("prow")
    pieces = lax.axis_size("pcol")
    capacity = rows_dev // (devices - 1) + 2
    block = -(-capacity // 16) * 16
    me = lax.axis_index("prow").astype(jnp.int32).reshape(1)
    col = lax.axis_index("pcol").astype(jnp.int32).reshape(1)
    piv = pivots.reshape(1, count)
    params = pltpu.CompilerParams(vmem_limit_bytes=VMEM_BYTES)
    smem = _whole(pltpu.SMEM)
    vmem = _whole()

    outgoing = pl.pallas_call(
        functools.partial(_outgoing_kernel, devices, block),
        out_shape=[jax.ShapeDtypeStruct((block, cols_dev), F32)] * devices,
        in_specs=[smem, vmem, vmem],
        out_specs=[vmem] * devices,
        compiler_params=params,
        name="outgoing_rows",
    )(me, piv, slab)

    def swap(x, axis, size, step):
        return lax.ppermute(x, axis, [(i, i ^ step) for i in range(size)])

    rows = [outgoing[0]] + [swap(outgoing[s], "prow", devices, s) for s in range(1, devices)]

    panels = [panel] + [swap(panel, "pcol", pieces, s) for s in range(1, pieces)]

    high, low, kept = pl.pallas_call(
        functools.partial(_factor_kernel, devices, block, pieces),
        out_shape=[
            jax.ShapeDtypeStruct((rows_dev, devices * block), BF16),
            jax.ShapeDtypeStruct((rows_dev, devices * block), BF16),
            jax.ShapeDtypeStruct((rows_dev, cols_dev), F32),
        ],
        in_specs=[smem, smem, vmem, vmem, vmem] + [vmem] * pieces,
        out_specs=[vmem] * 3,
        scratch_shapes=[pltpu.VMEM((rows_dev, count), F32)],
        compiler_params=params,
        name="left_factor",
    )(me, col, piv, slab, tri_inverse, *panels)

    return pl.pallas_call(
        functools.partial(_update_kernel, devices, block),
        out_shape=jax.ShapeDtypeStruct((rows_dev, cols_dev), F32),
        in_specs=[vmem] * (3 + devices),
        out_specs=vmem,
        scratch_shapes=[pltpu.VMEM((devices * block, cols_dev), BF16)] * 2,
        compiler_params=params,
        name="update",
    )(high, low, kept, *rows)


def solution(mesh):
    return jax.shard_map(
        per_device,
        mesh=mesh,
        in_specs=(P("prow", "pcol"), P("prow", "pcol"), P(), P()),
        out_specs=P("prow", "pcol"),
        check_vma=False,
    )
```

time: 136 us -> 47.1 us (0.35)
  the two profiles are of different devices: /device:TPU:0 before, /device:TPU:8 now
where the time goes in v1:
time: 47.1 us; the launch traced here: 46.9 us
  waiting for transfers between devices  23 us (49%)
  starting transfers between devices  12.1 us (26%)
  Pallas kernels  7.76 us (16%)
  local copies, waits for them, and re-layouts  4.08 us (9%)
    ppermute x10, waiting for transfers between devices, swap(): return lax.ppermute(x, axis, [(i, i ^ step) for i in range(size)])  23 us
    ppermute x10, starting transfers between devices, swap(): return lax.ppermute(x, axis, [(i, i ^ step) for i in range(size)])  12.1 us
    unnamed x10, local copies, waits for them, and re-layouts  4.08 us
    pallas_call x1, Pallas kernels, per_device(): pl.pallas_call(functools.partial(_factor_kernel, devices, block, pieces),...  3.48 us
    pallas_call x1, Pallas kernels, per_device(): pl.pallas_call(functools.partial(_update_kernel, devices, block), out_sha...  2.35 us
    pallas_call x1, Pallas kernels, per_device(): pl.pallas_call(functools.partial(_outgoing_kernel, devices, block), out_s...  1.93 us
  transfers between devices with their start and end apart: 10, of which 5 were waited for; matrix products, arithmetic and copies ran while one was open for 0% of the time, Pallas kernels for 12%

profile of v1, /device:TPU:8, one launch (start us, length us, event | category | flops | bytes accessed | tf_op | source)
XLA Modules:
  0.0 46.9 jit_solution(13007059675659456531)
XLA Ops:
  0.0 1.5 %collective-permute-start.1 = (f32[512,128]{1,0:T(8,128)}, f32[512,128]{1,0:T(8,128)S(1)}, u32[]{:S(2)}, u32[]{:S(2)}) collective-permute-start(f32[512,128]{1,0:T(8,128)} %refs_0_.1), channel_id=1, source_target_pairs={{0,2},{1,3},{2,0},{3,1},{4,6},{5,7},{6,4},{7,5},{8,10},{9,11},{10,... | collective-permute-start | bytes 786440 | tf_op jit(solution)/shard_map/ppermute | solution.py:166
  1.5 0.0 collective-permute-start
  1.5 0.6 %collective-permute-start.2 = (f32[512,128]{1,0:T(8,128)}, f32[512,128]{1,0:T(8,128)S(1)}, u32[]{:S(2)}, u32[]{:S(2)}) collective-permute-start(f32[512,128]{1,0:T(8,128)} %refs_0_.1), channel_id=1, source_target_pairs={{0,3},{1,2},{2,1},{3,0},{4,7},{5,6},{6,5},{7,4},{8,11},{9,10},{10,... | collective-permute-start | bytes 786440 | tf_op jit(solution)/shard_map/ppermute | solution.py:166
  2.1 0.0 copy-start.4
  2.1 0.7 %copy-done.4 = s32[512]{0:T(512)S(1)} copy-done((s32[512]{0:T(512)S(1)}, s32[512]{0:T(512)}, u32[]{:S(2)}) %copy-start.4) | copy-done | bytes 2072
  2.8 0.0 copy-start
  2.8 1.2 %copy-done = f32[512,512]{1,0:T(8,128)S(1)} copy-done((f32[512,512]{1,0:T(8,128)S(1)}, f32[512,512]{1,0:T(8,128)}, u32[]{:S(2)}) %copy-start) | copy-done | bytes 1048600
  4.0 0.0 copy-start.1
  4.1 1.9 %outgoing_rows.1 = (f32[80,512]{1,0:T(8,128)S(1)}, f32[80,512]{1,0:T(8,128)S(1)}, f32[80,512]{1,0:T(8,128)S(1)}, f32[80,512]{1,0:T(8,128)}, f32[80,512]{1,0:T(8,...) custom-call(s32[1]{0:T(128)} %bitcast.me_ref, s32[1,512]{1,0:T(1,128)S(1)} %bitcast.3, ...), custom_call_target="tpu_custom_call" | custom-call | tf_op jit(solution)/shard_map/outgoing_rows/pallas_call | solution.py:156
  6.0 1.5 %collective-permute-start.3 = (f32[80,512]{1,0:T(8,128)S(1)}, f32[80,512]{1,0:T(8,128)S(1)}, u32[]{:S(2)}, u32[]{:S(2)}) collective-permute-start(f32[80,512]{1,0:T(8,128)S(1)} %get-tuple-element.20), channel_id=1, source_target_pairs={{0,4},{4,0},{8,12},{12,8},{16,20},{20,16},{24,28},{28,24},{1,5},{5... | collective-permute-start | bytes 491528 | tf_op jit(solution)/shard_map/ppermute | solution.py:166
  7.5 0.5 collective-permute-start.4
  7.9 4.2 %collective-permute-done.3.refs_1_ = f32[80,512]{1,0:T(8,128)S(1)} collective-permute-done((f32[80,512]{1,0:T(8,128)S(1)}, f32[80,512]{1,0:T(8,128)S(1)}, u32[]{:S(2)}, u32[]{:S(2)}) %collective-permute-start.3) | collective-permute-done | bytes 163872 | tf_op jit(solution)/shard_map/ppermute | solution.py:166
  12.1 1.4 %collective-permute-start.5 = (f32[80,512]{1,0:T(8,128)}, f32[80,512]{1,0:T(8,128)S(1)}, u32[]{:S(2)}, u32[]{:S(2)}) collective-permute-start(f32[80,512]{1,0:T(8,128)} %get-tuple-element.22), channel_id=1, source_target_pairs={{0,12},{4,8},{8,4},{12,0},{16,28},{20,24},{24,20},{28,16},{1,13},{... | collective-permute-start | bytes 491528 | tf_op jit(solution)/shard_map/ppermute | solution.py:166
  13.5 0.0 collective-permute-done.4.refs_2_
  13.5 2.6 %collective-permute-start.6 = (f32[80,512]{1,0:T(8,128)}, f32[80,512]{1,0:T(8,128)S(1)}, u32[]{:S(2)}, u32[]{:S(2)}) collective-permute-start(f32[80,512]{1,0:T(8,128)} %get-tuple-element.23), channel_id=1, source_target_pairs={{0,16},{4,20},{8,24},{12,28},{16,0},{20,4},{24,8},{28,12},{1,17},{... | collective-permute-start | bytes 491528 | tf_op jit(solution)/shard_map/ppermute | solution.py:166
  16.1 0.0 collective-permute-done.1.refs_2_
  16.1 1.5 %collective-permute-start.7 = (f32[80,512]{1,0:T(8,128)}, f32[80,512]{1,0:T(8,128)S(1)}, u32[]{:S(2)}, u32[]{:S(2)}) collective-permute-start(f32[80,512]{1,0:T(8,128)} %get-tuple-element.24), channel_id=1, source_target_pairs={{0,20},{4,16},{8,28},{12,24},{16,4},{20,0},{24,12},{28,8},{1,21},{... | collective-permute-start | bytes 491528 | tf_op jit(solution)/shard_map/ppermute | solution.py:166
  17.6 0.0 collective-permute-done.refs_1_
  17.6 1.5 %collective-permute-start.8 = (f32[80,512]{1,0:T(8,128)S(1)}, f32[80,512]{1,0:T(8,128)S(1)}, u32[]{:S(2)}, u32[]{:S(2)}) collective-permute-start(f32[80,512]{1,0:T(8,128)S(1)} %get-tuple-element.25), channel_id=1, source_target_pairs={{0,24},{4,28},{8,16},{12,20},{16,8},{20,12},{24,0},{28,4},{1,25},{... | collective-permute-start | bytes 491528 | tf_op jit(solution)/shard_map/ppermute | solution.py:166
  19.1 0.0 collective-permute-done.2.refs_3_
  19.1 1.0 %collective-permute-start.9 = (f32[80,512]{1,0:T(8,128)S(1)}, f32[80,512]{1,0:T(8,128)S(1)}, u32[]{:S(2)}, u32[]{:S(2)}) collective-permute-start(f32[80,512]{1,0:T(8,128)S(1)} %get-tuple-element.26), channel_id=1, source_target_pairs={{0,28},{4,24},{8,20},{12,16},{16,12},{20,8},{24,4},{28,0},{1,29},{... | collective-permute-start | bytes 491528 | tf_op jit(solution)/shard_map/ppermute | solution.py:166
  20.1 0.0 copy-done.1
  20.1 0.0 copy-start.2
  20.1 1.2 %copy-done.2 = f32[512,512]{1,0:T(8,128)S(1)} copy-done((f32[512,512]{1,0:T(8,128)S(1)}, f32[512,512]{1,0:T(8,128)}, u32[]{:S(2)}) %copy-start.2) | copy-done | bytes 1048600
  21.3 0.0 copy-start.3
  21.3 0.9 %copy-done.3 = f32[512,128]{1,0:T(8,128)S(1)} copy-done((f32[512,128]{1,0:T(8,128)S(1)}, f32[512,128]{1,0:T(8,128)}, u32[]{:S(2)}) %copy-start.3) | copy-done | bytes 262168
  22.3 3.5 %left_factor.1 = (bf16[512,640]{1,0:T(8,128)(2,1)S(1)}, bf16[512,640]{1,0:T(8,128)(2,1)S(1)}, f32[512,512]{1,0:T(8,128)S(1)}) custom-call(s32[1]{0:T(128)} %bitcast.me_ref, s32[1]{0:T(128)} %bitcast.1.col_ref, s32[1,512]{1,0:T(1,128)S(1)} %bitcast.4, f32[512,512]{1,0:T(8,128)S(1)} %copy-done.1, f32[512,512]{1,0:T(8,128)S(1)} %copy-done.2, ...), custom_call_target="tpu_custom_call" | custom-call | tf_op jit(solution)/shard_map/left_factor/pallas_call | solution.py:172
  25.7 0.0 collective-permute-done.5.refs_3_
  25.8 8.7 %collective-permute-done.6.refs_4_ = f32[80,512]{1,0:T(8,128)S(1)} collective-permute-done((f32[80,512]{1,0:T(8,128)}, f32[80,512]{1,0:T(8,128)S(1)}, u32[]{:S(2)}, u32[]{:S(2)}) %collective-permute-start.6) | collective-permute-done | bytes 163872 | tf_op jit(solution)/shard_map/ppermute | solution.py:166
  34.5 3.5 %collective-permute-done.7.refs_5_ = f32[80,512]{1,0:T(8,128)S(1)} collective-permute-done((f32[80,512]{1,0:T(8,128)}, f32[80,512]{1,0:T(8,128)S(1)}, u32[]{:S(2)}, u32[]{:S(2)}) %collective-permute-start.7) | collective-permute-done | bytes 163872 | tf_op jit(solution)/shard_map/ppermute | solution.py:166
  38.0 4.5 %collective-permute-done.8.refs_6_ = f32[80,512]{1,0:T(8,128)S(1)} collective-permute-done((f32[80,512]{1,0:T(8,128)S(1)}, f32[80,512]{1,0:T(8,128)S(1)}, u32[]{:S(2)}, u32[]{:S(2)}) %collective-permute-start.8) | collective-permute-done | bytes 163872 | tf_op jit(solution)/shard_map/ppermute | solution.py:166
  42.5 2.1 %collective-permute-done.9.refs_7_ = f32[80,512]{1,0:T(8,128)S(1)} collective-permute-done((f32[80,512]{1,0:T(8,128)S(1)}, f32[80,512]{1,0:T(8,128)S(1)}, u32[]{:S(2)}, u32[]{:S(2)}) %collective-permute-start.9) | collective-permute-done | bytes 163872 | tf_op jit(solution)/shard_map/ppermute | solution.py:166
  44.5 2.4 %update.1 = f32[512,512]{1,0:T(8,128)} custom-call(bf16[512,640]{1,0:T(8,128)(2,1)S(1)} %get-tuple-element.16.high_ref, bf16[512,640]{1,0:T(8,128)(2,1)S(1)} %get-tuple-element.17.low_ref, f32[512,512]{1,0:T(8,128)S(1)} %get-tuple-element.18.kept_ref, f32[80,512]{1,0:T(8,128)S(1)} %get-tuple-element.19.refs_0_, ...), custom_call_target="tpu_custom_call" | custom-call | tf_op jit(solution)/shard_map/update/pallas_call | solution.py:186
Async XLA Ops:
  0.0 16.1 %collective-permute-start.1 = (f32[512,128]{1,0:T(8,128)}, f32[512,128]{1,0:T(8,128)S(1)}, u32[]{:S(2)}, u32[]{:S(2)}) collective-permute-start(f32[512,128]{1,0:T(8,128)} %refs_0_.1), channel_id=1, source_target_pairs={{0,2},{1,3},{2,0},{3,1},{4,6},{5,7},{6,4},{7,5},{8,10},{9,11},{10,... | collective-permute-start | bytes 786440 | tf_op jit(solution)/shard_map/ppermute | solution.py:166
  1.5 16.1 %collective-permute-start = (f32[512,128]{1,0:T(8,128)}, f32[512,128]{1,0:T(8,128)S(1)}, u32[]{:S(2)}, u32[]{:S(2)}) collective-permute-start(f32[512,128]{1,0:T(8,128)} %refs_0_.1), channel_id=1, source_target_pairs={{0,1},{1,0},{2,3},{3,2},{4,5},{5,4},{6,7},{7,6},{8,9},{9,8},{10,11... | collective-permute-start | bytes 786440 | tf_op jit(solution)/shard_map/ppermute | solution.py:166
  1.5 17.6 %collective-permute-start.2 = (f32[512,128]{1,0:T(8,128)}, f32[512,128]{1,0:T(8,128)S(1)}, u32[]{:S(2)}, u32[]{:S(2)}) collective-permute-start(f32[512,128]{1,0:T(8,128)} %refs_0_.1), channel_id=1, source_target_pairs={{0,3},{1,2},{2,1},{3,0},{4,7},{5,6},{6,5},{7,4},{8,11},{9,10},{10,... | collective-permute-start | bytes 786440 | tf_op jit(solution)/shard_map/ppermute | solution.py:166
  2.1 0.7 %copy-start.4 = (s32[512]{0:T(512)S(1)}, s32[512]{0:T(512)}, u32[]{:S(2)}) copy-start(s32[512]{0:T(512)} %param.7) | copy-start | bytes 6148
  2.8 1.2 %copy-start = (f32[512,512]{1,0:T(8,128)S(1)}, f32[512,512]{1,0:T(8,128)}, u32[]{:S(2)}) copy-start(f32[512,512]{1,0:T(8,128)} %slab_ref.3) | copy-start | bytes 3145732
  4.0 16.0 %copy-start.1 = (f32[512,512]{1,0:T(8,128)S(1)}, f32[512,512]{1,0:T(8,128)}, u32[]{:S(2)}) copy-start(f32[512,512]{1,0:T(8,128)} %slab_ref.3) | copy-start | bytes 3145732
  6.0 6.1 %collective-permute-start.3 = (f32[80,512]{1,0:T(8,128)S(1)}, f32[80,512]{1,0:T(8,128)S(1)}, u32[]{:S(2)}, u32[]{:S(2)}) collective-permute-start(f32[80,512]{1,0:T(8,128)S(1)} %get-tuple-element.20), channel_id=1, source_target_pairs={{0,4},{4,0},{8,12},{12,8},{16,20},{20,16},{24,28},{28,24},{1,5},{5... | collective-permute-start | bytes 491528 | tf_op jit(solution)/shard_map/ppermute | solution.py:166
  7.5 6.0 %collective-permute-start.4 = (f32[80,512]{1,0:T(8,128)S(1)}, f32[80,512]{1,0:T(8,128)S(1)}, u32[]{:S(2)}, u32[]{:S(2)}) collective-permute-start(f32[80,512]{1,0:T(8,128)S(1)} %get-tuple-element.21), channel_id=1, source_target_pairs={{0,8},{4,12},{8,0},{12,4},{16,24},{20,28},{24,16},{28,20},{1,9},{5... | collective-permute-start | bytes 491528 | tf_op jit(solution)/shard_map/ppermute | solution.py:166
  12.1 13.7 %collective-permute-start.5 = (f32[80,512]{1,0:T(8,128)}, f32[80,512]{1,0:T(8,128)S(1)}, u32[]{:S(2)}, u32[]{:S(2)}) collective-permute-start(f32[80,512]{1,0:T(8,128)} %get-tuple-element.22), channel_id=1, source_target_pairs={{0,12},{4,8},{8,4},{12,0},{16,28},{20,24},{24,20},{28,16},{1,13},{... | collective-permute-start | bytes 491528 | tf_op jit(solution)/shard_map/ppermute | solution.py:166
  13.5 21.0 %collective-permute-start.6 = (f32[80,512]{1,0:T(8,128)}, f32[80,512]{1,0:T(8,128)S(1)}, u32[]{:S(2)}, u32[]{:S(2)}) collective-permute-start(f32[80,512]{1,0:T(8,128)} %get-tuple-element.23), channel_id=1, source_target_pairs={{0,16},{4,20},{8,24},{12,28},{16,0},{20,4},{24,8},{28,12},{1,17},{... | collective-permute-start | bytes 491528 | tf_op jit(solution)/shard_map/ppermute | solution.py:166
  16.1 21.9 %collective-permute-start.7 = (f32[80,512]{1,0:T(8,128)}, f32[80,512]{1,0:T(8,128)S(1)}, u32[]{:S(2)}, u32[]{:S(2)}) collective-permute-start(f32[80,512]{1,0:T(8,128)} %get-tuple-element.24), channel_id=1, source_target_pairs={{0,20},{4,16},{8,28},{12,24},{16,4},{20,0},{24,12},{28,8},{1,21},{... | collective-permute-start | bytes 491528 | tf_op jit(solution)/shard_map/ppermute | solution.py:166
  17.6 24.9 %collective-permute-start.8 = (f32[80,512]{1,0:T(8,128)S(1)}, f32[80,512]{1,0:T(8,128)S(1)}, u32[]{:S(2)}, u32[]{:S(2)}) collective-permute-start(f32[80,512]{1,0:T(8,128)S(1)} %get-tuple-element.25), channel_id=1, source_target_pairs={{0,24},{4,28},{8,16},{12,20},{16,8},{20,12},{24,0},{28,4},{1,25},{... | collective-permute-start | bytes 491528 | tf_op jit(solution)/shard_map/ppermute | solution.py:166
  19.1 25.5 %collective-permute-start.9 = (f32[80,512]{1,0:T(8,128)S(1)}, f32[80,512]{1,0:T(8,128)S(1)}, u32[]{:S(2)}, u32[]{:S(2)}) collective-permute-start(f32[80,512]{1,0:T(8,128)S(1)} %get-tuple-element.26), channel_id=1, source_target_pairs={{0,28},{4,24},{8,20},{12,16},{16,12},{20,8},{24,4},{28,0},{1,29},{... | collective-permute-start | bytes 491528 | tf_op jit(solution)/shard_map/ppermute | solution.py:166
  20.1 1.2 %copy-start.2 = (f32[512,512]{1,0:T(8,128)S(1)}, f32[512,512]{1,0:T(8,128)}, u32[]{:S(2)}) copy-start(f32[512,512]{1,0:T(8,128)} %tri_ref.1) | copy-start | bytes 3145732
  21.3 0.9 %copy-start.3 = (f32[512,128]{1,0:T(8,128)S(1)}, f32[512,128]{1,0:T(8,128)}, u32[]{:S(2)}) copy-start(f32[512,128]{1,0:T(8,128)} %refs_0_.1) | copy-start | bytes 786436

commit v2 on v1

v2 whole, which is shorter than its diff:
```python
import functools

import jax
import jax.numpy as jnp
from jax import lax
from jax.experimental import pallas as pl
from jax.experimental.pallas import tpu as pltpu
from jax.sharding import PartitionSpec as P

F32 = jnp.float32
BF16 = jnp.bfloat16
VMEM_BYTES = 24 * 1024 * 1024
LOAD_PARTS = 4
STORE_PARTS = 4
ASSEMBLE_FLOPS = 20_000_000_000


def _two_parts(x):
    high = x.astype(BF16)
    low = (x - high.astype(F32)).astype(BF16)
    return high, low


def _dot(a, b):
    return jnp.dot(a, b, preferred_element_type=F32)


def _dot_nt(a, b):
    return lax.dot_general(a, b, (((1,), (1,)), ((), ())), preferred_element_type=F32)


def _iota(shape, dim):
    return lax.broadcasted_iota(jnp.int32, shape, dim)


def _owners_and_ranks(piv, rows_dev, devices):
    count = piv.shape[1]
    owner = piv // rows_dev
    local = piv - owner * rows_dev
    is_owner = _iota((devices, count), 0) == owner
    earlier = (_iota((count, count), 0) < _iota((count, count), 1)).astype(BF16)
    ranks = _dot(is_owner.astype(BF16), earlier)
    rank = jnp.sum(jnp.where(is_owner, ranks, 0.0), axis=0, keepdims=True)
    return owner, local, rank.astype(jnp.int32)


def _select_rows(one_hot, parts):
    high, low = parts
    return _dot(one_hot, high) + _dot(one_hot, low)


def _outgoing_kernel(devices, block, me_ref, piv_hbm, slab_hbm, *refs):
    out_refs = refs[:devices]
    piv_ref, slab_ref, sems = refs[devices:]
    me = me_ref[0]
    rows_dev = slab_ref.shape[0]
    part = rows_dev // LOAD_PARTS
    piv_copy = pltpu.make_async_copy(piv_hbm, piv_ref, sems.at[0])
    piv_copy.start()
    loads = []
    for i in range(LOAD_PARTS):
        rows = pl.ds(i * part, part)
        loads.append(pltpu.make_async_copy(slab_hbm.at[rows], slab_ref.at[rows], sems.at[1 + i]))
        loads[-1].start()
    piv_copy.wait()
    piv = piv_ref[...]
    count = piv.shape[1]
    owner, local, rank = _owners_and_ranks(piv, rows_dev, devices)
    for load in loads:
        load.wait()
    parts = _two_parts(slab_ref[...])

    @pl.when(me == 0)
    def _():
        total = (devices - 1) * block
        slot = (owner - 1) * block + rank
        pick = (_iota((total, count), 0) == slot).astype(BF16)
        if count < rows_dev:
            pick = jnp.pad(pick, ((0, 0), (0, rows_dev - count)))
        rows = _select_rows(pick, parts)
        for step in range(1, devices):
            out_refs[step][...] = rows[(step - 1) * block : step * block]
        out_refs[0][...] = jnp.zeros_like(out_refs[0])

    @pl.when(me != 0)
    def _():
        slot = jnp.where(owner == me, rank, -1)
        pick = (_iota((block, count), 0) == slot).astype(BF16)
        at_row = (_iota((rows_dev, count), 0) == local).astype(BF16)
        mine = _select_rows(_dot_nt(pick, at_row).astype(BF16), parts)
        for step in range(devices):
            out_refs[step][...] = mine


def _relay_kernel(step, me_ref, came_ref, own_ref, out_ref):
    me = me_ref[0]
    instead = (me == 0) | (me == step)

    @pl.when(instead)
    def _():
        out_ref[...] = own_ref[...]

    @pl.when(jnp.logical_not(instead))
    def _():
        out_ref[...] = came_ref[...]


def _factor_kernel(devices, block, order, early, pieces, me_ref, col_ref, piv_ref, slab_ref, tri_ref, *refs):
    panel_refs = refs[:pieces]
    high_early, low_early, high_late, low_late, kept_ref, panel_rel, tri_rel, w_ref = refs[pieces:]
    me = me_ref[0]
    rows_dev = slab_ref.shape[0]
    depth = panel_refs[0].shape[1]
    piv = piv_ref[...]
    count = piv.shape[1]
    owner, local, rank = _owners_and_ranks(piv, rows_dev, devices)

    @pl.when(me == 0)
    def _():
        w_ref[...] = tri_ref[...]

    @pl.when(me != 0)
    def _():
        for step in range(pieces):
            first = pl.multiple_of((col_ref[0] ^ step) * depth, depth)
            tri_rel[pl.ds(step * depth, depth), :] = tri_ref[pl.ds(first, depth), :]
            panel_rel[:, pl.ds(step * depth, depth)] = panel_refs[step][...]
        tri_high, tri_low = _two_parts(tri_rel[...])
        high, low = _two_parts(panel_rel[...])
        w_ref[...] = -((_dot(high, tri_low) + _dot(low, tri_high)) + _dot(high, tri_high))

    total = devices * block
    relative = owner ^ me
    slot = rank
    lead_first = 0
    for place, step in enumerate(order):
        slot = jnp.where(relative == step, rank + place * block, slot)
        lead_first = jnp.where(me == step, place * block, lead_first)
    place = (_iota((total, count), 0) == slot).astype(BF16)
    is_mine = owner == me
    lead_slot = jnp.where(is_mine, lead_first + rank, -1)
    lead = (_iota((total, count), 0) == lead_slot).astype(BF16)
    at_row = ((_iota((rows_dev, count), 0) == local) & is_mine).astype(F32)
    high, low = _two_parts(w_ref[...])
    at_row_bf16 = at_row.astype(BF16)
    split = early * block
    for rows, high_ref, low_ref in ((slice(0, split), high_early, low_early), (slice(split, total), high_late, low_late)):
        high_ref[...] = (_dot_nt(high, place[rows]) + _dot_nt(at_row_bf16, lead[rows])).astype(BF16)
        low_ref[...] = _dot_nt(low, place[rows]).astype(BF16)
    taken = jnp.sum(at_row, axis=1, keepdims=True)
    stays = (taken < 0.5) & (me != 0)
    kept_ref[...] = jnp.where(stays, slab_ref[...], 0.0)


def _split_rows(block, block_refs, high_rows, low_rows):
    for step, ref in enumerate(block_refs):
        high, low = _two_parts(ref[...])
        high_rows[pl.ds(step * block, block), :] = high
        low_rows[pl.ds(step * block, block), :] = low


def _product(high, low, high_rows, low_rows):
    return (_dot(high, low_rows) + _dot(low, high_rows)) + _dot(high, high_rows)


def _assemble_kernel(block, blocks, *refs):
    high_rows, low_rows = refs[blocks:]
    _split_rows(block, refs[:blocks], high_rows, low_rows)


def _early_kernel(high_ref, low_ref, kept_ref, high_rows, low_rows, out_ref):
    out_ref[...] = kept_ref[...] + _product(high_ref[...], low_ref[...], high_rows[...], low_rows[...])


def _late_kernel(block, blocks, high_ref, low_ref, base_ref, *refs):
    out_hbm, high_rows, low_rows, result, sems = refs[blocks:]
    _split_rows(block, refs[:blocks], high_rows, low_rows)
    high, low = high_rows[...], low_rows[...]
    part = result.shape[0] // STORE_PARTS
    stores = []
    for i in range(STORE_PARTS):
        rows = pl.ds(i * part, part)
        result[rows, :] = base_ref[rows, :] + _product(high_ref[rows, :], low_ref[rows, :], high, low)
        stores.append(pltpu.make_async_copy(result.at[rows], out_hbm.at[rows], sems.at[i]))
        stores[-1].start()
    for store in stores:
        store.wait()


def per_device(slab, panel, tri_inverse, pivots):
    rows_dev, cols_dev = slab.shape
    count = pivots.shape[0]
    devices = lax.axis_size("prow")
    pieces = lax.axis_size("pcol")
    capacity = rows_dev // (devices - 1) + 2
    block = -(-capacity // 16) * 16
    me = lax.axis_index("prow").astype(jnp.int32).reshape(1)
    col = lax.axis_index("pcol").astype(jnp.int32).reshape(1)
    piv = pivots.reshape(1, count)
    params = pltpu.CompilerParams(vmem_limit_bytes=VMEM_BYTES)
    smem = pl.BlockSpec(memory_space=pltpu.SMEM)
    vmem = pl.BlockSpec(memory_space=pltpu.VMEM)
    hbm = pl.BlockSpec(memory_space=pltpu.HBM)
    rows_type = jax.ShapeDtypeStruct((block, cols_dev), F32)

    outgoing = pl.pallas_call(
        functools.partial(_outgoing_kernel, devices, block),
        out_shape=[rows_type] * devices,
        in_specs=[smem, hbm, hbm],
        out_specs=[vmem] * devices,
        scratch_shapes=[
            pltpu.VMEM((1, count), jnp.int32),
            pltpu.VMEM((rows_dev, cols_dev), F32),
            pltpu.SemaphoreType.DMA((LOAD_PARTS + 1,)),
        ],
        compiler_params=params,
        name="outgoing_rows",
    )(me, piv, slab)

    def swap(x, axis, size, step):
        return lax.ppermute(x, axis, [(i, i ^ step) for i in range(size)])

    relayed = list(range(4, devices, 2))
    direct = [1, 2] + relayed + [3]
    rows = {0: outgoing[0]}
    for step in direct:
        rows[step] = swap(outgoing[step], "prow", devices, step)
    for step in relayed:
        other = step ^ 1
        passed = pl.pallas_call(
            functools.partial(_relay_kernel, step),
            out_shape=rows_type,
            in_specs=[smem, vmem, vmem],
            out_specs=vmem,
            compiler_params=params,
            name="relay",
        )(me, rows[step], outgoing[other])
        pairs = [(i, i ^ 1) for i in range(devices) if i not in (0, step)] + [(0, other), (step, 1)]
        rows[other] = lax.ppermute(passed, "prow", pairs)
    order = [0] + direct + [step ^ 1 for step in relayed]
    early = 1 + len(direct)
    late = devices - early

    panels = {0: panel}
    for step in range(2, pieces, 2):
        panels[step] = swap(panels[0], "pcol", pieces, step)
    for step in range(0, pieces, 2):
        panels[step ^ 1] = swap(panels[step], "pcol", pieces, 1)

    high_early, low_early, high_late, low_late, kept = pl.pallas_call(
        functools.partial(_factor_kernel, devices, block, order, early, pieces),
        out_shape=[jax.ShapeDtypeStruct((rows_dev, k * block), BF16) for k in (early, early, late, late)]
        + [jax.ShapeDtypeStruct((rows_dev, cols_dev), F32)],
        in_specs=[smem, smem, vmem, vmem, vmem] + [vmem] * pieces,
        out_specs=[vmem] * 5,
        scratch_shapes=[
            pltpu.VMEM((rows_dev, count), F32),
            pltpu.VMEM((count, count), F32),
            pltpu.VMEM((rows_dev, count), F32),
        ],
        compiler_params=params,
        name="left_factor",
    )(me, col, piv, slab, tri_inverse, *[panels[s] for s in range(pieces)])

    result_type = jax.ShapeDtypeStruct((rows_dev, cols_dev), F32)
    high_rows, low_rows = pl.pallas_call(
        functools.partial(_assemble_kernel, block, early),
        out_shape=[jax.ShapeDtypeStruct((early * block, cols_dev), BF16)] * 2,
        in_specs=[vmem] * early,
        out_specs=[vmem] * 2,
        compiler_params=params,
        cost_estimate=pl.CostEstimate(flops=ASSEMBLE_FLOPS, bytes_accessed=0, transcendentals=0),
        name="assemble_rows",
    )(*[rows[s] for s in order[:early]])
    partial = pl.pallas_call(
        _early_kernel,
        out_shape=result_type,
        in_specs=[vmem] * 5,
        out_specs=vmem,
        compiler_params=params,
        name="early_rows",
    )(high_early, low_early, kept, high_rows, low_rows)
    return pl.pallas_call(
        functools.partial(_late_kernel, block, late),
        out_shape=result_type,
        in_specs=[vmem] * (3 + late),
        out_specs=hbm,
        scratch_shapes=[pltpu.VMEM((late * block, cols_dev), BF16)] * 2
        + [pltpu.VMEM((rows_dev, cols_dev), F32), pltpu.SemaphoreType.DMA((STORE_PARTS,))],
        compiler_params=params,
        name="late_rows",
    )(high_late, low_late, partial, *[rows[s] for s in order[early:]])


def solution(mesh):
    return jax.shard_map(
        per_device,
        mesh=mesh,
        in_specs=(P("prow", "pcol"), P("prow", "pcol"), P(), P()),
        out_specs=P("prow", "pcol"),
        check_vma=False,
    )
```

time: 47.1 us -> 34.7 us (0.74)
  the two profiles are of different devices: /device:TPU:8 before, /device:TPU:0 now
where the time goes in v2:
time: 34.7 us; the launch traced here: 34.5 us
  starting transfers between devices  15.1 us (44%)
  waiting for transfers between devices  11.7 us (34%)
  Pallas kernels  5.45 us (16%)
  local copies, waits for them, and re-layouts  2.13 us (6%)
    ppermute x8, starting transfers between devices, swap(): return lax.ppermute(x, axis, [(i, i ^ step) for i in range(size)])  9.81 us
    ppermute x8, waiting for transfers between devices, swap(): return lax.ppermute(x, axis, [(i, i ^ step) for i in range(size)])  8.68 us
    ppermute x2, starting transfers between devices, per_device(): rows[other] = lax.ppermute(passed, 'prow', pairs)  5.28 us
    ppermute x2, waiting for transfers between devices, per_device(): rows[other] = lax.ppermute(passed, 'prow', pairs)  3.06 us
    unnamed x10, local copies, waits for them, and re-layouts  2.13 us
    pallas_call x1, Pallas kernels, per_device(): pl.pallas_call(functools.partial(_factor_kernel, devices, block, order, e...  1.74 us
    pallas_call x1, Pallas kernels, per_device(): pl.pallas_call(functools.partial(_late_kernel, block, late), out_shape=re...  1.3 us
    pallas_call x1, Pallas kernels, per_device(): pl.pallas_call(functools.partial(_outgoing_kernel, devices, block), out_s...  1.27 us
  transfers between devices with their start and end apart: 10, of which 3 were waited for; matrix products, arithmetic and copies ran while one was open for 0% of the time, Pallas kernels for 8%

profile of v2, /device:TPU:0, one launch (start us, length us, event | category | flops | bytes accessed | tf_op | source)
XLA Modules:
  0.0 34.5 jit_solution(6885660414608483226)
XLA Ops:
  0.0 0.0 copy-start.4
  0.0 0.7 %copy-done.4 = s32[512]{0:T(512)S(1)} copy-done((s32[512]{0:T(512)S(1)}, s32[512]{0:T(512)}, u32[]{:S(2)}) %copy-start.4) | copy-done | bytes 2072
  0.7 0.0 copy-start
  0.7 1.2 %copy-done = f32[512,512]{1,0:T(8,128)S(1)} copy-done((f32[512,512]{1,0:T(8,128)S(1)}, f32[512,512]{1,0:T(8,128)}, u32[]{:S(2)}) %copy-start) | copy-done | bytes 1048600
  1.9 0.0 copy-start.3
  1.9 1.3 %outgoing_rows.1 = (f32[80,512]{1,0:T(8,128)S(1)}, f32[80,512]{1,0:T(8,128)S(1)}, f32[80,512]{1,0:T(8,128)S(1)}, f32[80,512]{1,0:T(8,128)S(1)}, f32[80,512]{1,0:...) custom-call(s32[1]{0:T(128)} %bitcast.me_ref, s32[1,512]{1,0:T(1,128)S(1)} %bitcast.3, ...), custom_call_target="tpu_custom_call" | custom-call | tf_op jit(solution)/shard_map/outgoing_rows/pallas_call | solution.py:206
  3.2 4.0 %collective-permute-start.5 = (f32[80,512]{1,0:T(8,128)S(1)}, f32[80,512]{1,0:T(8,128)S(1)}, u32[]{:S(2)}, u32[]{:S(2)}) collective-permute-start(f32[80,512]{1,0:T(8,128)S(1)} %get-tuple-element.28), channel_id=1, source_target_pairs={{0,16},{4,20},{8,24},{12,28},{16,0},{20,4},{24,8},{28,12},{1,17},{... | collective-permute-start | bytes 491528 | tf_op jit(solution)/shard_map/ppermute | solution.py:221
  7.1 0.0 copy-done.3
  7.1 1.5 %collective-permute-start.1 = (f32[512,128]{1,0:T(8,128)S(1)}, f32[512,128]{1,0:T(8,128)S(1)}, u32[]{:S(2)}, u32[]{:S(2)}) collective-permute-start(f32[512,128]{1,0:T(8,128)S(1)} %copy-done.3), channel_id=1, source_target_pairs={{0,2},{1,3},{2,0},{3,1},{4,6},{5,7},{6,4},{7,5},{8,10},{9,11},{10,... | collective-permute-start | bytes 786440 | tf_op jit(solution)/shard_map/ppermute | solution.py:221
  8.7 1.3 %collective-permute-start.6 = (f32[80,512]{1,0:T(8,128)S(1)}, f32[80,512]{1,0:T(8,128)S(1)}, u32[]{:S(2)}, u32[]{:S(2)}) collective-permute-start(f32[80,512]{1,0:T(8,128)S(1)} %get-tuple-element.29), channel_id=1, source_target_pairs={{0,24},{4,28},{8,16},{12,20},{16,8},{20,12},{24,0},{28,4},{1,25},{... | collective-permute-start | bytes 491528 | tf_op jit(solution)/shard_map/ppermute | solution.py:221
  10.0 1.5 %collective-permute-start.3 = (f32[80,512]{1,0:T(8,128)S(1)}, f32[80,512]{1,0:T(8,128)S(1)}, u32[]{:S(2)}, u32[]{:S(2)}) collective-permute-start(f32[80,512]{1,0:T(8,128)S(1)} %get-tuple-element.26), channel_id=1, source_target_pairs={{0,4},{4,0},{8,12},{12,8},{16,20},{20,16},{24,28},{28,24},{1,5},{5... | collective-permute-start | bytes 491528 | tf_op jit(solution)/shard_map/ppermute | solution.py:221
  11.5 0.2 collective-permute-start.4
  11.7 7.5 %collective-permute-done.5.refs_3_.came_ref = f32[80,512]{1,0:T(8,128)S(1)} collective-permute-done((f32[80,512]{1,0:T(8,128)S(1)}, f32[80,512]{1,0:T(8,128)S(1)}, u32[]{:S(2)}, u32[]{:S(2)}) %collective-permute-start.5) | collective-permute-done | bytes 163872 | tf_op jit(solution)/shard_map/ppermute | solution.py:221
  19.2 0.9 %collective-permute-start.7 = (f32[80,512]{1,0:T(8,128)S(1)}, f32[80,512]{1,0:T(8,128)S(1)}, u32[]{:S(2)}, u32[]{:S(2)}) collective-permute-start(f32[80,512]{1,0:T(8,128)S(1)} %get-tuple-element.30), channel_id=1, source_target_pairs={{0,12},{4,8},{8,4},{12,0},{16,28},{20,24},{24,20},{28,16},{1,13},{... | collective-permute-start | bytes 491528 | tf_op jit(solution)/shard_map/ppermute | solution.py:221
  20.2 0.0 collective-permute-done.6.refs_4_.came_ref
  20.2 0.1 collective-permute-start
  20.3 0.0 collective-permute-done.3.refs_1_
  20.3 5.3 %collective-permute-start.8 = (f32[80,512]{1,0:T(8,128)S(1)}, f32[80,512]{1,0:T(8,128)S(1)}, u32[]{:S(2)}, u32[]{:S(2)}) collective-permute-start(f32[80,512]{1,0:T(8,128)S(1)} %relay.2), channel_id=1, source_target_pairs={{4,0},{8,12},{12,8},{20,16},{24,28},{28,24},{0,20},{16,4},{5,1},{9... | collective-permute-start | bytes 491528 | tf_op jit(solution)/shard_map/ppermute | solution.py:239
  25.6 0.0 collective-permute-done.4.refs_2_
  25.6 0.0 collective-permute-start.9
  25.6 0.0 collective-permute-done.1.refs_2_
  25.6 0.3 collective-permute-start.2
  25.9 0.0 collective-permute-done.7.refs_5_
  25.9 0.0 copy-start.1
  25.9 0.0 copy-start.2
  25.9 0.1 assemble_rows.1
  26.0 0.0 collective-permute-done.refs_1_
  26.0 1.2 %collective-permute-done.2.refs_3_ = f32[512,128]{1,0:T(8,128)S(1)} collective-permute-done((f32[512,128]{1,0:T(8,128)S(1)}, f32[512,128]{1,0:T(8,128)S(1)}, u32[]{:S(2)}, u32[]{:S(2)}) %collective-permute-start.2) | collective-permute-done | bytes 262176 | tf_op jit(solution)/shard_map/ppermute | solution.py:221
  27.2 0.0 copy-done.1
  27.2 0.2 copy-done.2
  27.4 1.7 %left_factor.1 = (bf16[512,480]{1,0:T(8,128)(2,1)S(1)}, bf16[512,480]{1,0:T(8,128)(2,1)S(1)}, bf16[512,160]{1,0:T(8,128)(2,1)S(1)}, bf16[512,160]{1,0:T(8,128)(2,1)S(1)}, f32[512,512]{1,0:T(8,128)S(1)}) custom-call(s32[1]{0:T(128)} %bitcast.me_ref, s32[1]{0:T(128)} %bitcast.1.col_ref, s32[1,512]{1,0:T(1,128)S(1)} %bitcast.4, f32[512,512]{1,0:T(8,128)S(1)} %copy-done.1, ...), custom_call_target="tpu_custom_call" | custom-call | tf_op jit(solution)/shard_map/left_factor/pallas_call | solution.py:250
  29.2 1.0 %early_rows.1.base_ref = f32[512,512]{1,0:T(8,128)S(1)} custom-call(bf16[512,480]{1,0:T(8,128)(2,1)S(1)} %get-tuple-element.22.high_ref, bf16[512,480]{1,0:T(8,128)(2,1)S(1)} %get-tuple-element.23.low_ref, f32[512,512]{1,0:T(8,128)S(1)} %get-tuple-element.24.kept_ref, bf16[480,512]{1,0:T(8,128)(2,1)S(1)} %get-tuple-element.31.high_rows, ...), custom_call_target="tpu_custom_call" | custom-call | tf_op jit(solution)/shard_map/early_rows/pallas_call | solution.py:275
  30.1 0.0 collective-permute-done.8.refs_0_
  30.1 3.1 %collective-permute-done.9.refs_1_ = f32[80,512]{1,0:T(8,128)S(1)} collective-permute-done((f32[80,512]{1,0:T(8,128)S(1)}, f32[80,512]{1,0:T(8,128)S(1)}, u32[]{:S(2)}, u32[]{:S(2)}) %collective-permute-start.9) | collective-permute-done | bytes 163872 | tf_op jit(solution)/shard_map/ppermute | solution.py:239
  33.2 1.3 %late_rows.1 = f32[512,512]{1,0:T(8,128)} custom-call(bf16[512,160]{1,0:T(8,128)(2,1)S(1)} %get-tuple-element.20.high_ref, bf16[512,160]{1,0:T(8,128)(2,1)S(1)} %get-tuple-element.21.low_ref, f32[512,512]{1,0:T(8,128)S(1)} %early_rows.1.base_ref, f32[80,512]{1,0:T(8,128)S(1)} %collective-permute-done.8.refs_0_, f32[80,512]{1,0:T(8,128)S(1)} %collective-permute-done.9.refs_1_), custom_call_target="tpu_custom_call" | custom-call | tf_op jit(solution)/shard_map/late_rows/pallas_call | solution.py:283
  (2 shorter events, 0.0 us)
Async XLA Ops:
  0.0 0.7 %copy-start.4 = (s32[512]{0:T(512)S(1)}, s32[512]{0:T(512)}, u32[]{:S(2)}) copy-start(s32[512]{0:T(512)} %param.7) | copy-start | bytes 6148
  0.7 1.2 %copy-start = (f32[512,512]{1,0:T(8,128)S(1)}, f32[512,512]{1,0:T(8,128)}, u32[]{:S(2)}) copy-start(f32[512,512]{1,0:T(8,128)} %slab_hbm.1) | copy-start | bytes 3145732
  1.9 5.2 %copy-start.3 = (f32[512,128]{1,0:T(8,128)S(1)}, f32[512,128]{1,0:T(8,128)}, u32[]{:S(2)}) copy-start(f32[512,128]{1,0:T(8,128)} %refs_0_.1) | copy-start | bytes 786436
  3.2 16.1 %collective-permute-start.5 = (f32[80,512]{1,0:T(8,128)S(1)}, f32[80,512]{1,0:T(8,128)S(1)}, u32[]{:S(2)}, u32[]{:S(2)}) collective-permute-start(f32[80,512]{1,0:T(8,128)S(1)} %get-tuple-element.28), channel_id=1, source_target_pairs={{0,16},{4,20},{8,24},{12,28},{16,0},{20,4},{24,8},{28,12},{1,17},{... | collective-permute-start | bytes 491528 | tf_op jit(solution)/shard_map/ppermute | solution.py:221
  7.1 18.4 %collective-permute-start.1 = (f32[512,128]{1,0:T(8,128)S(1)}, f32[512,128]{1,0:T(8,128)S(1)}, u32[]{:S(2)}, u32[]{:S(2)}) collective-permute-start(f32[512,128]{1,0:T(8,128)S(1)} %copy-done.3), channel_id=1, source_target_pairs={{0,2},{1,3},{2,0},{3,1},{4,6},{5,7},{6,4},{7,5},{8,10},{9,11},{10,... | collective-permute-start | bytes 786440 | tf_op jit(solution)/shard_map/ppermute | solution.py:221
  8.7 11.5 %collective-permute-start.6 = (f32[80,512]{1,0:T(8,128)S(1)}, f32[80,512]{1,0:T(8,128)S(1)}, u32[]{:S(2)}, u32[]{:S(2)}) collective-permute-start(f32[80,512]{1,0:T(8,128)S(1)} %get-tuple-element.29), channel_id=1, source_target_pairs={{0,24},{4,28},{8,16},{12,20},{16,8},{20,12},{24,0},{28,4},{1,25},{... | collective-permute-start | bytes 491528 | tf_op jit(solution)/shard_map/ppermute | solution.py:221
  10.0 10.3 %collective-permute-start.3 = (f32[80,512]{1,0:T(8,128)S(1)}, f32[80,512]{1,0:T(8,128)S(1)}, u32[]{:S(2)}, u32[]{:S(2)}) collective-permute-start(f32[80,512]{1,0:T(8,128)S(1)} %get-tuple-element.26), channel_id=1, source_target_pairs={{0,4},{4,0},{8,12},{12,8},{16,20},{20,16},{24,28},{28,24},{1,5},{5... | collective-permute-start | bytes 491528 | tf_op jit(solution)/shard_map/ppermute | solution.py:221
  11.5 14.1 %collective-permute-start.4 = (f32[80,512]{1,0:T(8,128)S(1)}, f32[80,512]{1,0:T(8,128)S(1)}, u32[]{:S(2)}, u32[]{:S(2)}) collective-permute-start(f32[80,512]{1,0:T(8,128)S(1)} %get-tuple-element.27), channel_id=1, source_target_pairs={{0,8},{4,12},{8,0},{12,4},{16,24},{20,28},{24,16},{28,20},{1,9},{5... | collective-permute-start | bytes 491528 | tf_op jit(solution)/shard_map/ppermute | solution.py:221
  19.2 6.6 %collective-permute-start.7 = (f32[80,512]{1,0:T(8,128)S(1)}, f32[80,512]{1,0:T(8,128)S(1)}, u32[]{:S(2)}, u32[]{:S(2)}) collective-permute-start(f32[80,512]{1,0:T(8,128)S(1)} %get-tuple-element.30), channel_id=1, source_target_pairs={{0,12},{4,8},{8,4},{12,0},{16,28},{20,24},{24,20},{28,16},{1,13},{... | collective-permute-start | bytes 491528 | tf_op jit(solution)/shard_map/ppermute | solution.py:221
  20.2 5.8 %collective-permute-start = (f32[512,128]{1,0:T(8,128)S(1)}, f32[512,128]{1,0:T(8,128)S(1)}, u32[]{:S(2)}, u32[]{:S(2)}) collective-permute-start(f32[512,128]{1,0:T(8,128)S(1)} %copy-done.3), channel_id=1, source_target_pairs={{0,1},{1,0},{2,3},{3,2},{4,5},{5,4},{6,7},{7,6},{8,9},{9,8},{10,11... | collective-permute-start | bytes 786440 | tf_op jit(solution)/shard_map/ppermute | solution.py:221
  20.3 9.8 %collective-permute-start.8 = (f32[80,512]{1,0:T(8,128)S(1)}, f32[80,512]{1,0:T(8,128)S(1)}, u32[]{:S(2)}, u32[]{:S(2)}) collective-permute-start(f32[80,512]{1,0:T(8,128)S(1)} %relay.2), channel_id=1, source_target_pairs={{4,0},{8,12},{12,8},{20,16},{24,28},{28,24},{0,20},{16,4},{5,1},{9... | collective-permute-start | bytes 491528 | tf_op jit(solution)/shard_map/ppermute | solution.py:239
  25.6 7.6 %collective-permute-start.9 = (f32[80,512]{1,0:T(8,128)S(1)}, f32[80,512]{1,0:T(8,128)S(1)}, u32[]{:S(2)}, u32[]{:S(2)}) collective-permute-start(f32[80,512]{1,0:T(8,128)S(1)} %relay.3), channel_id=1, source_target_pairs={{4,0},{8,12},{12,8},{16,20},{20,16},{28,24},{0,28},{24,4},{5,1},{9... | collective-permute-start | bytes 491528 | tf_op jit(solution)/shard_map/ppermute | solution.py:239
  25.6 1.6 %collective-permute-start.2 = (f32[512,128]{1,0:T(8,128)S(1)}, f32[512,128]{1,0:T(8,128)S(1)}, u32[]{:S(2)}, u32[]{:S(2)}) collective-permute-start(f32[512,128]{1,0:T(8,128)S(1)} %collective-permute-done.1.refs_2_), channel_id=1, source_target_pairs={{0,1},{1,0},{2,3},{3,2},{4,5},{5,4},{6,7},{7,6},{8,9},{9,8},{10,11... | collective-permute-start | bytes 786440 | tf_op jit(solution)/shard_map/ppermute | solution.py:221
  25.9 1.3 %copy-start.1 = (f32[512,512]{1,0:T(8,128)S(1)}, f32[512,512]{1,0:T(8,128)}, u32[]{:S(2)}) copy-start(f32[512,512]{1,0:T(8,128)} %slab_hbm.1) | copy-start | bytes 3145732
  25.9 1.5 %copy-start.2 = (f32[512,512]{1,0:T(8,128)S(1)}, f32[512,512]{1,0:T(8,128)}, u32[]{:S(2)}) copy-start(f32[512,512]{1,0:T(8,128)} %tri_ref.1) | copy-start | bytes 3145732
